TPU v7x, 512 devices: a whole 4x8x8 slice. The times are simulated.
512 devices in a mesh: ctx: 64 (over y, x, core), head: 8 (over z).
Axes of the slice: x: 4, y: 8, z: 8, core: 2. Of those that a mesh axis runs over, the one named last changes fastest.
Arguments:
- query_proj: bfloat16 [16384, 3072], P('ctx', 'head'), may hold values from -150 to 150
- key_proj: bfloat16 [16384, 3072], P('ctx', 'head'), may hold values from -150 to 150
- value: bfloat16 [16384, 3072], P('ctx', 'head'), may hold values from -6 to 6
- out_grad: bfloat16 [16384, 3072], P('ctx', 'head'), may hold values from -6 to 6
- query_gain: float32 [3072], P('head'), may hold values from 0.5 to 1.5
- key_gain: float32 [3072], P('head'), may hold values from 0.5 to 1.5
- band_bias: float32 [7, 24], P(None, 'head'), may hold values from -1.5 to 1.5
- tile_mask: int32 [128, 7, 2], P('ctx'), may hold values from 0 to 1, as said below
Outputs:
- attended: bfloat16 [16384, 3072], P('ctx', 'head')
- query_grad: bfloat16 [16384, 3072], P('ctx', 'head')
- key_grad: bfloat16 [16384, 3072], P('ctx', 'head')
- value_grad: bfloat16 [16384, 3072], P('ctx', 'head')
Inputs may be any that keep to these rules, and one draw needn't show every extreme that they name: Every entry of band 0 is 1. For b >= 1 the mask is symmetric between the two slabs of a band: tile_mask[i * 2 + r, b, t] equals tile_mask[j * 2 + t, b, r] where j = i XOR 2 ** (b - 1). Farther bands hold fewer live tiles.
All inputs are finite; a program needn't handle non-finite values.
Results may differ from a plain program's by a relative error of at most 0.03.
Values may be sent and summed in bfloat16 or wider, within the bound.
A program may use at most 64 MiB of HBM per device.

v0:
```python
import jax
import jax.numpy as jnp
from jax import lax
from jax.sharding import PartitionSpec as P

HD = 128
TILE = 128


epsilon = 1e-06
neg_fill = -1e30


def swapped(block, axis, stride):
    count = lax.axis_size(axis)
    route = []
    for low in range(count):
        high = low | 1 << stride
        if high != low and high < count:
            route += [(low, high), (high, low)]
    return lax.ppermute(block, axis, route)


def expand(tiles):
    return jnp.repeat(jnp.repeat(tiles, TILE, axis=0), TILE, axis=1) > 0


def split_heads(matrix):
    return matrix.reshape(matrix.shape[0], -1, HD)


def grad_terms(probs, query_heads, key_heads, value_heads, grad_heads, row_delta):
    value_part = jnp.einsum("hqk,qhd->khd", probs, grad_heads, preferred_element_type=jnp.float32)
    prob_grad = jnp.einsum(
        "qhd,khd->hqk", grad_heads, value_heads, preferred_element_type=jnp.float32
    )
    score_grad = (probs.astype(jnp.float32) * (prob_grad - row_delta[:, :, None])).astype(
        jnp.bfloat16
    )
    query_part = jnp.einsum(
        "hqk,khd->qhd", score_grad, key_heads, preferred_element_type=jnp.float32
    )
    key_part = jnp.einsum(
        "hqk,qhd->khd", score_grad, query_heads, preferred_element_type=jnp.float32
    )
    return (query_part, key_part, value_part)


def on_device(query_proj, key_proj, value, out_grad, query_gain, key_gain, band_bias, tile_mask):
    score_scale = HD ** (-0.5)
    rows = query_proj.shape[0]
    width = query_proj.shape[1] * lax.axis_size("head")
    query_vals = query_proj.astype(jnp.float32)
    key_vals = key_proj.astype(jnp.float32)
    query_sq, key_sq = lax.psum(
        (
            jnp.sum(query_vals * query_vals, axis=1, keepdims=True),
            jnp.sum(key_vals * key_vals, axis=1, keepdims=True),
        ),
        "head",
    )
    query_factor = lax.rsqrt(query_sq / width + epsilon)
    key_factor = lax.rsqrt(key_sq / width + epsilon)
    query_n = (query_vals * query_factor * query_gain).astype(jnp.bfloat16)
    key_n = (key_vals * key_factor * key_gain).astype(jnp.bfloat16)
    levels = lax.axis_size("ctx").bit_length() - 1
    query_heads = split_heads(query_n)
    grad_heads = split_heads(out_grad)
    key_heads = split_heads(key_n)
    value_heads = split_heads(value)
    key_list = [key_heads]
    value_list = [value_heads]
    for band_bit in range(levels):
        far_key, far_value = swapped((key_n, value), "ctx", band_bit)
        key_list.append(split_heads(far_key))
        value_list.append(split_heads(far_value))
    masked = []
    for band in range(levels + 1):
        scores = jnp.einsum(
            "qhd,khd->hqk", query_heads, key_list[band], preferred_element_type=jnp.float32
        )
        scores = scores * score_scale + band_bias[band][:, None, None]
        masked.append(jnp.where(expand(tile_mask[:, band, :])[None], scores, neg_fill))
    row_top = masked[0].max(axis=2)
    for scores in masked[1:]:
        row_top = jnp.maximum(row_top, scores.max(axis=2))
    row_total = jnp.zeros_like(row_top)
    for scores in masked:
        row_total = row_total + jnp.exp(scores - row_top[:, :, None]).sum(axis=2)
    log_norm = row_top + jnp.log(row_total)
    probs_list = [jnp.exp(scores - log_norm[:, :, None]).astype(jnp.bfloat16) for scores in masked]
    output = jnp.zeros(query_heads.shape, jnp.float32)
    for band in range(levels + 1):
        output = output + jnp.einsum(
            "hqk,khd->qhd", probs_list[band], value_list[band], preferred_element_type=jnp.float32
        )
    attended = output.reshape(rows, -1).astype(jnp.bfloat16)
    row_delta = jnp.sum(
        grad_heads.astype(jnp.float32) * split_heads(attended).astype(jnp.float32), axis=2
    ).T
    query_acc, key_acc, value_acc = grad_terms(
        probs_list[0], query_heads, key_heads, value_heads, grad_heads, row_delta
    )
    for band_bit in range(levels):
        query_part, key_part, value_part = grad_terms(
            probs_list[band_bit + 1],
            query_heads,
            key_list[band_bit + 1],
            value_list[band_bit + 1],
            grad_heads,
            row_delta,
        )
        query_acc = query_acc + query_part
        key_back, value_back = (
            swapped(key_part.reshape(rows, -1).astype(jnp.bfloat16), "ctx", band_bit).astype(
                jnp.float32
            ),
            swapped(value_part.reshape(rows, -1).astype(jnp.bfloat16), "ctx", band_bit).astype(
                jnp.float32
            ),
        )
        key_acc = key_acc + key_back.reshape(key_acc.shape)
        value_acc = value_acc + value_back.reshape(value_acc.shape)
    query_ngrad = (query_acc * score_scale).reshape(rows, -1)
    key_ngrad = (key_acc * score_scale).reshape(rows, -1)
    query_scaled = query_gain * query_ngrad
    key_scaled = key_gain * key_ngrad
    query_inner, key_inner = lax.psum(
        (
            jnp.sum(query_scaled * query_vals, axis=1, keepdims=True),
            jnp.sum(key_scaled * key_vals, axis=1, keepdims=True),
        ),
        "head",
    )
    query_grad = (
        query_factor * query_scaled - query_vals * query_factor**3 * (query_inner / width)
    ).astype(jnp.bfloat16)
    key_grad = (key_factor * key_scaled - key_vals * key_factor**3 * (key_inner / width)).astype(
        jnp.bfloat16
    )
    return (attended, query_grad, key_grad, value_acc.reshape(rows, -1).astype(jnp.bfloat16))


def solution(mesh):
    placed = (
        P("ctx", "head"),
        P("ctx", "head"),
        P("ctx", "head"),
        P("ctx", "head"),
        P("head"),
        P("head"),
        P(None, "head"),
        P("ctx", None, None),
    )
    return jax.shard_map(
        on_device,
        mesh=mesh,
        in_specs=placed,
        out_specs=(P("ctx", "head"), P("ctx", "head"), P("ctx", "head"), P("ctx", "head")),
        check_vma=False,
    )
```

profile of v0, /device:TPU:6, one launch (start us, length us, event | category | flops | bytes accessed | tf_op | source)
XLA Modules:
  0.0 200.7 jit_solution(15376680798209793129)
XLA Ops:
  2.9 23.2 %all-reduce.1 = (f32[256,1]{0,1:T(1,128)S(1)}, f32[256,1]{0,1:T(1,128)S(1)}) all-reduce(f32[256,1]{0,1:T(1,128)S(1)} %bitcast.356, f32[256,1]{0,1:T(1,128)S(1)} %bitcast.357), channel_id=1, replica_groups=mesh['ctx'=64,'head'=8] {'head'}, use_global_device_ids=true, to_apply=%region_1.0 | all-reduce | flops 512 | bytes 4096 | tf_op jit(solution)/shard_map/psum | solution.py:55
  27.5 7.7 %collective-permute-start.5 = (bf16[256,384]{0,1:T(8,128)(2,1)S(1)}, bf16[256,384]{0,1:T(8,128)(2,1)S(1)}, u32[]{:S(2)}, u32[]{:S(2)}) collective-permute-start(bf16[256,384]{0,1:T(8,128)(2,1)S(1)} %fusion.47), channel_id=1, source_target_pairs={{0,256},{256,0},{8,264},{264,8},{16,272},{272,16},{24,280},{280,24... | collective-permute-start | bytes 589832 | tf_op jit(solution)/shard_map/ppermute | solution.py:21
  35.2 2.7 %collective-permute-start.4 = (bf16[256,384]{0,1:T(8,128)(2,1)S(1)}, bf16[256,384]{0,1:T(8,128)(2,1)S(1)}, u32[]{:S(2)}, u32[]{:S(2)}) collective-permute-start(bf16[256,384]{0,1:T(8,128)(2,1)S(1)} %fusion.47), channel_id=1, source_target_pairs={{0,128},{128,0},{8,136},{136,8},{16,144},{144,16},{24,152},{152,24... | collective-permute-start | bytes 589832 | tf_op jit(solution)/shard_map/ppermute | solution.py:21
  37.9 2.6 %collective-permute-start.3 = (bf16[256,384]{0,1:T(8,128)(2,1)S(1)}, bf16[256,384]{0,1:T(8,128)(2,1)S(1)}, u32[]{:S(2)}, u32[]{:S(2)}) collective-permute-start(bf16[256,384]{0,1:T(8,128)(2,1)S(1)} %fusion.47), channel_id=1, source_target_pairs={{0,64},{64,0},{8,72},{72,8},{16,80},{80,16},{24,88},{88,24},{32,96... | collective-permute-start | bytes 589832 | tf_op jit(solution)/shard_map/ppermute | solution.py:21
  40.5 3.3 %collective-permute-start.2 = (bf16[256,384]{0,1:T(8,128)(2,1)S(1)}, bf16[256,384]{0,1:T(8,128)(2,1)S(1)}, u32[]{:S(2)}, u32[]{:S(2)}) collective-permute-start(bf16[256,384]{0,1:T(8,128)(2,1)S(1)} %fusion.47), channel_id=1, source_target_pairs={{0,32},{32,0},{8,40},{40,8},{16,48},{48,16},{24,56},{56,24},{64,96... | collective-permute-start | bytes 589832 | tf_op jit(solution)/shard_map/ppermute | solution.py:21
  53.7 2.4 %collective-permute-start.6 = (bf16[256,384]{1,0:T(8,128)(2,1)}, bf16[256,384]{1,0:T(8,128)(2,1)}, u32[]{:S(2)}, u32[]{:S(2)}) collective-permute-start(bf16[256,384]{1,0:T(8,128)(2,1)} %param.10), channel_id=1, source_target_pairs={{0,8},{8,0},{16,24},{24,16},{32,40},{40,32},{48,56},{56,48},{64,72... | collective-permute-start | bytes 589832 | tf_op jit(solution)/shard_map/ppermute | solution.py:21
  56.5 5.2 %collective-permute-start.8 = (bf16[256,384]{1,0:T(8,128)(2,1)}, bf16[256,384]{1,0:T(8,128)(2,1)}, u32[]{:S(2)}, u32[]{:S(2)}) collective-permute-start(bf16[256,384]{1,0:T(8,128)(2,1)} %param.10), channel_id=1, source_target_pairs={{0,32},{32,0},{8,40},{40,8},{16,48},{48,16},{24,56},{56,24},{64,96... | collective-permute-start | bytes 589832 | tf_op jit(solution)/shard_map/ppermute | solution.py:21
  62.1 3.3 %collective-permute-start.9 = (bf16[256,384]{1,0:T(8,128)(2,1)}, bf16[256,384]{1,0:T(8,128)(2,1)}, u32[]{:S(2)}, u32[]{:S(2)}) collective-permute-start(bf16[256,384]{1,0:T(8,128)(2,1)} %param.10), channel_id=1, source_target_pairs={{0,64},{64,0},{8,72},{72,8},{16,80},{80,16},{24,88},{88,24},{32,96... | collective-permute-start | bytes 589832 | tf_op jit(solution)/shard_map/ppermute | solution.py:21
  65.8 4.0 %collective-permute-start.10 = (bf16[256,384]{1,0:T(8,128)(2,1)}, bf16[256,384]{1,0:T(8,128)(2,1)}, u32[]{:S(2)}, u32[]{:S(2)}) collective-permute-start(bf16[256,384]{1,0:T(8,128)(2,1)} %param.10), channel_id=1, source_target_pairs={{0,128},{128,0},{8,136},{136,8},{16,144},{144,16},{24,152},{152,24... | collective-permute-start | bytes 589832 | tf_op jit(solution)/shard_map/ppermute | solution.py:21
  70.2 2.0 %collective-permute-start.11 = (bf16[256,384]{1,0:T(8,128)(2,1)}, bf16[256,384]{1,0:T(8,128)(2,1)}, u32[]{:S(2)}, u32[]{:S(2)}) collective-permute-start(bf16[256,384]{1,0:T(8,128)(2,1)} %param.10), channel_id=1, source_target_pairs={{0,256},{256,0},{8,264},{264,8},{16,272},{272,16},{24,280},{280,24... | collective-permute-start | bytes 589832 | tf_op jit(solution)/shard_map/ppermute | solution.py:21
  99.3 2.1 %convolution_add_fusion.1 = f32[3,256,128]{1,2,0:T(8,128)} fusion(f32[3,256,128]{1,2,0:T(8,128)} %fusion.66, bf16[256,3,128]{0,2,1:T(8,128)(2,1)} %bitcast.298, bf16[3,256,256]{1,2,0:T(8,128)(2,1)S(1)} %get-tuple-element.35), kind=kOutput, calls=%fused_computation.45 | convolution fusion | flops 50429952 | bytes 1376256 | tf_op jit(solution)/shard_map/hqk,khd->qhd/dot_general | solution.py:94
  104.1 2.5 %multiply_reduce_fusion = (f32[256,3]{0,1:T(4,128)S(1)}, bf16[3,256,128]{1,2,0:T(8,128)(2,1)}) fusion(bf16[256,3,128]{0,2,1:T(8,128)(2,1)S(1)} %bitcast.264, f32[3,256,128]{1,2,0:T(8,128)} %fusion.70, f32[3,256,128]{1,2,0:T(8,128)} %fusion.69, f32[3,256,128]{1,2,0:T(8,128)} %fusion.68, f32[3,256,128]{1,2,0:T(8,128)} %fusion.67, ...), kind=kOutput, calls=%fused_computation.122 | convolution fusion | flops 51313920 | bytes 2952192 | tf_op jit(solution)/shard_map/hqk,khd->qhd/dot_general | solution.py:94
  118.0 3.9 %collective-permute-start.19 = (bf16[256,384]{0,1:T(8,128)(2,1)}, bf16[256,384]{0,1:T(8,128)(2,1)}, u32[]{:S(2)}, u32[]{:S(2)}) collective-permute-start(bf16[256,384]{0,1:T(8,128)(2,1)} %bitcast.70), channel_id=1, source_target_pairs={{0,16},{16,0},{8,24},{24,8},{32,48},{48,32},{40,56},{56,40},{64,80... | collective-permute-start | bytes 589832 | tf_op jit(solution)/shard_map/ppermute | solution.py:21
  121.9 2.5 %collective-permute-start.20 = (bf16[256,384]{0,1:T(8,128)(2,1)}, bf16[256,384]{0,1:T(8,128)(2,1)}, u32[]{:S(2)}, u32[]{:S(2)}) collective-permute-start(bf16[256,384]{0,1:T(8,128)(2,1)} %bitcast.73), channel_id=1, source_target_pairs={{0,32},{32,0},{8,40},{40,8},{16,48},{48,16},{24,56},{56,24},{64,96... | collective-permute-start | bytes 589832 | tf_op jit(solution)/shard_map/ppermute | solution.py:21
  124.5 3.5 %collective-permute-start.21 = (bf16[256,384]{0,1:T(8,128)(2,1)}, bf16[256,384]{0,1:T(8,128)(2,1)}, u32[]{:S(2)}, u32[]{:S(2)}) collective-permute-start(bf16[256,384]{0,1:T(8,128)(2,1)} %bitcast.76), channel_id=1, source_target_pairs={{0,64},{64,0},{8,72},{72,8},{16,80},{80,16},{24,88},{88,24},{32,96... | collective-permute-start | bytes 589832 | tf_op jit(solution)/shard_map/ppermute | solution.py:21
  127.9 4.7 %collective-permute-start.22 = (bf16[256,384]{0,1:T(8,128)(2,1)}, bf16[256,384]{0,1:T(8,128)(2,1)}, u32[]{:S(2)}, u32[]{:S(2)}) collective-permute-start(bf16[256,384]{0,1:T(8,128)(2,1)} %bitcast.79), channel_id=1, source_target_pairs={{0,128},{128,0},{8,136},{136,8},{16,144},{144,16},{24,152},{152,24... | collective-permute-start | bytes 589832 | tf_op jit(solution)/shard_map/ppermute | solution.py:21
  140.3 5.0 %collective-permute-start.23 = (bf16[256,384]{0,1:T(8,128)(2,1)S(1)}, bf16[256,384]{0,1:T(8,128)(2,1)S(1)}, u32[]{:S(2)}, u32[]{:S(2)}) collective-permute-start(bf16[256,384]{0,1:T(8,128)(2,1)S(1)} %bitcast.314), channel_id=1, source_target_pairs={{0,256},{256,0},{8,264},{264,8},{16,272},{272,16},{24,280},{280,24... | collective-permute-start | bytes 589832 | tf_op jit(solution)/shard_map/ppermute | solution.py:21
  145.3 3.5 %collective-permute-start.13 = (bf16[256,384]{0,1:T(8,128)(2,1)S(1)}, bf16[256,384]{0,1:T(8,128)(2,1)S(1)}, u32[]{:S(2)}, u32[]{:S(2)}) collective-permute-start(bf16[256,384]{0,1:T(8,128)(2,1)S(1)} %bitcast.319), channel_id=1, source_target_pairs={{0,16},{16,0},{8,24},{24,8},{32,48},{48,32},{40,56},{56,40},{64,80... | collective-permute-start | bytes 589832 | tf_op jit(solution)/shard_map/ppermute | solution.py:21
  151.7 4.1 %collective-permute-start.14 = (bf16[256,384]{0,1:T(8,128)(2,1)S(1)}, bf16[256,384]{0,1:T(8,128)(2,1)S(1)}, u32[]{:S(2)}, u32[]{:S(2)}) collective-permute-start(bf16[256,384]{0,1:T(8,128)(2,1)S(1)} %bitcast.315), channel_id=1, source_target_pairs={{0,32},{32,0},{8,40},{40,8},{16,48},{48,16},{24,56},{56,24},{64,96... | collective-permute-start | bytes 589832 | tf_op jit(solution)/shard_map/ppermute | solution.py:21
  155.8 3.2 %collective-permute-start.15 = (bf16[256,384]{0,1:T(8,128)(2,1)S(1)}, bf16[256,384]{0,1:T(8,128)(2,1)S(1)}, u32[]{:S(2)}, u32[]{:S(2)}) collective-permute-start(bf16[256,384]{0,1:T(8,128)(2,1)S(1)} %bitcast.316), channel_id=1, source_target_pairs={{0,64},{64,0},{8,72},{72,8},{16,80},{80,16},{24,88},{88,24},{32,96... | collective-permute-start | bytes 589832 | tf_op jit(solution)/shard_map/ppermute | solution.py:21
  159.1 4.0 %collective-permute-start.16 = (bf16[256,384]{0,1:T(8,128)(2,1)S(1)}, bf16[256,384]{0,1:T(8,128)(2,1)S(1)}, u32[]{:S(2)}, u32[]{:S(2)}) collective-permute-start(bf16[256,384]{0,1:T(8,128)(2,1)S(1)} %bitcast.318), channel_id=1, source_target_pairs={{0,128},{128,0},{8,136},{136,8},{16,144},{144,16},{24,152},{152,24... | collective-permute-start | bytes 589832 | tf_op jit(solution)/shard_map/ppermute | solution.py:21
  163.1 2.0 %collective-permute-start.17 = (bf16[256,384]{0,1:T(8,128)(2,1)}, bf16[256,384]{0,1:T(8,128)(2,1)}, u32[]{:S(2)}, u32[]{:S(2)}) collective-permute-start(bf16[256,384]{0,1:T(8,128)(2,1)} %bitcast.59), channel_id=1, source_target_pairs={{0,256},{256,0},{8,264},{264,8},{16,272},{272,16},{24,280},{280,24... | collective-permute-start | bytes 589832 | tf_op jit(solution)/shard_map/ppermute | solution.py:21
  167.5 13.8 %collective-permute-done.16 = bf16[256,384]{0,1:T(8,128)(2,1)S(1)} collective-permute-done((bf16[256,384]{0,1:T(8,128)(2,1)S(1)}, bf16[256,384]{0,1:T(8,128)(2,1)S(1)}, u32[]{:S(2)}, u32[]{:S(2)}) %collective-permute-start.16) | collective-permute-done | bytes 196640 | tf_op jit(solution)/shard_map/ppermute | solution.py:21
  183.3 14.1 %all-reduce = (f32[256,1]{0,1:T(1,128)S(1)}, f32[256,1]{0,1:T(1,128)S(1)}) all-reduce(f32[256,1]{0,1:T(1,128)S(1)} %bitcast.346, f32[256,1]{0,1:T(1,128)S(1)} %bitcast.358), channel_id=1, replica_groups=mesh['ctx'=64,'head'=8] {'head'}, use_global_device_ids=true, to_apply=%region_20.21 | all-reduce | flops 512 | bytes 4096 | tf_op jit(solution)/shard_map/psum | solution.py:128
  (211 shorter events, 73.8 us)
Async XLA Ops:
  27.5 23.9 %collective-permute-start.5 = (bf16[256,384]{0,1:T(8,128)(2,1)S(1)}, bf16[256,384]{0,1:T(8,128)(2,1)S(1)}, u32[]{:S(2)}, u32[]{:S(2)}) collective-permute-start(bf16[256,384]{0,1:T(8,128)(2,1)S(1)} %fusion.47), channel_id=1, source_target_pairs={{0,256},{256,0},{8,264},{264,8},{16,272},{272,16},{24,280},{280,24... | collective-permute-start | bytes 589832 | tf_op jit(solution)/shard_map/ppermute | solution.py:21
  35.2 18.5 %collective-permute-start.4 = (bf16[256,384]{0,1:T(8,128)(2,1)S(1)}, bf16[256,384]{0,1:T(8,128)(2,1)S(1)}, u32[]{:S(2)}, u32[]{:S(2)}) collective-permute-start(bf16[256,384]{0,1:T(8,128)(2,1)S(1)} %fusion.47), channel_id=1, source_target_pairs={{0,128},{128,0},{8,136},{136,8},{16,144},{144,16},{24,152},{152,24... | collective-permute-start | bytes 589832 | tf_op jit(solution)/shard_map/ppermute | solution.py:21
  37.9 18.6 %collective-permute-start.3 = (bf16[256,384]{0,1:T(8,128)(2,1)S(1)}, bf16[256,384]{0,1:T(8,128)(2,1)S(1)}, u32[]{:S(2)}, u32[]{:S(2)}) collective-permute-start(bf16[256,384]{0,1:T(8,128)(2,1)S(1)} %fusion.47), channel_id=1, source_target_pairs={{0,64},{64,0},{8,72},{72,8},{16,80},{80,16},{24,88},{88,24},{32,96... | collective-permute-start | bytes 589832 | tf_op jit(solution)/shard_map/ppermute | solution.py:21
  40.5 21.6 %collective-permute-start.2 = (bf16[256,384]{0,1:T(8,128)(2,1)S(1)}, bf16[256,384]{0,1:T(8,128)(2,1)S(1)}, u32[]{:S(2)}, u32[]{:S(2)}) collective-permute-start(bf16[256,384]{0,1:T(8,128)(2,1)S(1)} %fusion.47), channel_id=1, source_target_pairs={{0,32},{32,0},{8,40},{40,8},{16,48},{48,16},{24,56},{56,24},{64,96... | collective-permute-start | bytes 589832 | tf_op jit(solution)/shard_map/ppermute | solution.py:21
  43.8 22.0 %collective-permute-start = (bf16[256,384]{0,1:T(8,128)(2,1)S(1)}, bf16[256,384]{0,1:T(8,128)(2,1)S(1)}, u32[]{:S(2)}, u32[]{:S(2)}) collective-permute-start(bf16[256,384]{0,1:T(8,128)(2,1)S(1)} %fusion.47), channel_id=1, source_target_pairs={{0,8},{8,0},{16,24},{24,16},{32,40},{40,32},{48,56},{56,48},{64,72... | collective-permute-start | bytes 589832 | tf_op jit(solution)/shard_map/ppermute | solution.py:21
  51.3 18.9 %collective-permute-start.1 = (bf16[256,384]{0,1:T(8,128)(2,1)S(1)}, bf16[256,384]{0,1:T(8,128)(2,1)S(1)}, u32[]{:S(2)}, u32[]{:S(2)}) collective-permute-start(bf16[256,384]{0,1:T(8,128)(2,1)S(1)} %fusion.47), channel_id=1, source_target_pairs={{0,16},{16,0},{8,24},{24,8},{32,48},{48,32},{40,56},{56,40},{64,80... | collective-permute-start | bytes 589832 | tf_op jit(solution)/shard_map/ppermute | solution.py:21
  53.7 43.9 %collective-permute-start.6 = (bf16[256,384]{1,0:T(8,128)(2,1)}, bf16[256,384]{1,0:T(8,128)(2,1)}, u32[]{:S(2)}, u32[]{:S(2)}) collective-permute-start(bf16[256,384]{1,0:T(8,128)(2,1)} %param.10), channel_id=1, source_target_pairs={{0,8},{8,0},{16,24},{24,16},{32,40},{40,32},{48,56},{56,48},{64,72... | collective-permute-start | bytes 589832 | tf_op jit(solution)/shard_map/ppermute | solution.py:21
  56.5 20.7 %collective-permute-start.8 = (bf16[256,384]{1,0:T(8,128)(2,1)}, bf16[256,384]{1,0:T(8,128)(2,1)}, u32[]{:S(2)}, u32[]{:S(2)}) collective-permute-start(bf16[256,384]{1,0:T(8,128)(2,1)} %param.10), channel_id=1, source_target_pairs={{0,32},{32,0},{8,40},{40,8},{16,48},{48,16},{24,56},{56,24},{64,96... | collective-permute-start | bytes 589832 | tf_op jit(solution)/shard_map/ppermute | solution.py:21
  62.1 21.6 %collective-permute-start.9 = (bf16[256,384]{1,0:T(8,128)(2,1)}, bf16[256,384]{1,0:T(8,128)(2,1)}, u32[]{:S(2)}, u32[]{:S(2)}) collective-permute-start(bf16[256,384]{1,0:T(8,128)(2,1)} %param.10), channel_id=1, source_target_pairs={{0,64},{64,0},{8,72},{72,8},{16,80},{80,16},{24,88},{88,24},{32,96... | collective-permute-start | bytes 589832 | tf_op jit(solution)/shard_map/ppermute | solution.py:21
  65.8 22.5 %collective-permute-start.10 = (bf16[256,384]{1,0:T(8,128)(2,1)}, bf16[256,384]{1,0:T(8,128)(2,1)}, u32[]{:S(2)}, u32[]{:S(2)}) collective-permute-start(bf16[256,384]{1,0:T(8,128)(2,1)} %param.10), channel_id=1, source_target_pairs={{0,128},{128,0},{8,136},{136,8},{16,144},{144,16},{24,152},{152,24... | collective-permute-start | bytes 589832 | tf_op jit(solution)/shard_map/ppermute | solution.py:21
  70.2 22.7 %collective-permute-start.11 = (bf16[256,384]{1,0:T(8,128)(2,1)}, bf16[256,384]{1,0:T(8,128)(2,1)}, u32[]{:S(2)}, u32[]{:S(2)}) collective-permute-start(bf16[256,384]{1,0:T(8,128)(2,1)} %param.10), channel_id=1, source_target_pairs={{0,256},{256,0},{8,264},{264,8},{16,272},{272,16},{24,280},{280,24... | collective-permute-start | bytes 589832 | tf_op jit(solution)/shard_map/ppermute | solution.py:21
  77.2 25.1 %collective-permute-start.7 = (bf16[256,384]{1,0:T(8,128)(2,1)}, bf16[256,384]{1,0:T(8,128)(2,1)}, u32[]{:S(2)}, u32[]{:S(2)}) collective-permute-start(bf16[256,384]{1,0:T(8,128)(2,1)} %param.10), channel_id=1, source_target_pairs={{0,16},{16,0},{8,24},{24,8},{32,48},{48,32},{40,56},{56,40},{64,80... | collective-permute-start | bytes 589832 | tf_op jit(solution)/shard_map/ppermute | solution.py:21
  116.1 23.5 %collective-permute-start.18 = (bf16[256,384]{0,1:T(8,128)(2,1)}, bf16[256,384]{0,1:T(8,128)(2,1)}, u32[]{:S(2)}, u32[]{:S(2)}) collective-permute-start(bf16[256,384]{0,1:T(8,128)(2,1)} %bitcast.67), channel_id=1, source_target_pairs={{0,8},{8,0},{16,24},{24,16},{32,40},{40,32},{48,56},{56,48},{64,72... | collective-permute-start | bytes 589832 | tf_op jit(solution)/shard_map/ppermute | solution.py:21
  118.0 27.3 %collective-permute-start.19 = (bf16[256,384]{0,1:T(8,128)(2,1)}, bf16[256,384]{0,1:T(8,128)(2,1)}, u32[]{:S(2)}, u32[]{:S(2)}) collective-permute-start(bf16[256,384]{0,1:T(8,128)(2,1)} %bitcast.70), channel_id=1, source_target_pairs={{0,16},{16,0},{8,24},{24,8},{32,48},{48,32},{40,56},{56,40},{64,80... | collective-permute-start | bytes 589832 | tf_op jit(solution)/shard_map/ppermute | solution.py:21
  121.9 27.8 %collective-permute-start.20 = (bf16[256,384]{0,1:T(8,128)(2,1)}, bf16[256,384]{0,1:T(8,128)(2,1)}, u32[]{:S(2)}, u32[]{:S(2)}) collective-permute-start(bf16[256,384]{0,1:T(8,128)(2,1)} %bitcast.73), channel_id=1, source_target_pairs={{0,32},{32,0},{8,40},{40,8},{16,48},{48,16},{24,56},{56,24},{64,96... | collective-permute-start | bytes 589832 | tf_op jit(solution)/shard_map/ppermute | solution.py:21
  124.5 27.2 %collective-permute-start.21 = (bf16[256,384]{0,1:T(8,128)(2,1)}, bf16[256,384]{0,1:T(8,128)(2,1)}, u32[]{:S(2)}, u32[]{:S(2)}) collective-permute-start(bf16[256,384]{0,1:T(8,128)(2,1)} %bitcast.76), channel_id=1, source_target_pairs={{0,64},{64,0},{8,72},{72,8},{16,80},{80,16},{24,88},{88,24},{32,96... | collective-permute-start | bytes 589832 | tf_op jit(solution)/shard_map/ppermute | solution.py:21
  127.9 27.9 %collective-permute-start.22 = (bf16[256,384]{0,1:T(8,128)(2,1)}, bf16[256,384]{0,1:T(8,128)(2,1)}, u32[]{:S(2)}, u32[]{:S(2)}) collective-permute-start(bf16[256,384]{0,1:T(8,128)(2,1)} %bitcast.79), channel_id=1, source_target_pairs={{0,128},{128,0},{8,136},{136,8},{16,144},{144,16},{24,152},{152,24... | collective-permute-start | bytes 589832 | tf_op jit(solution)/shard_map/ppermute | solution.py:21
  140.3 18.8 %collective-permute-start.23 = (bf16[256,384]{0,1:T(8,128)(2,1)S(1)}, bf16[256,384]{0,1:T(8,128)(2,1)S(1)}, u32[]{:S(2)}, u32[]{:S(2)}) collective-permute-start(bf16[256,384]{0,1:T(8,128)(2,1)S(1)} %bitcast.314), channel_id=1, source_target_pairs={{0,256},{256,0},{8,264},{264,8},{16,272},{272,16},{24,280},{280,24... | collective-permute-start | bytes 589832 | tf_op jit(solution)/shard_map/ppermute | solution.py:21
  145.3 17.8 %collective-permute-start.13 = (bf16[256,384]{0,1:T(8,128)(2,1)S(1)}, bf16[256,384]{0,1:T(8,128)(2,1)S(1)}, u32[]{:S(2)}, u32[]{:S(2)}) collective-permute-start(bf16[256,384]{0,1:T(8,128)(2,1)S(1)} %bitcast.319), channel_id=1, source_target_pairs={{0,16},{16,0},{8,24},{24,8},{32,48},{48,32},{40,56},{56,40},{64,80... | collective-permute-start | bytes 589832 | tf_op jit(solution)/shard_map/ppermute | solution.py:21
  149.8 17.7 %collective-permute-start.12 = (bf16[256,384]{0,1:T(8,128)(2,1)S(1)}, bf16[256,384]{0,1:T(8,128)(2,1)S(1)}, u32[]{:S(2)}, u32[]{:S(2)}) collective-permute-start(bf16[256,384]{0,1:T(8,128)(2,1)S(1)} %bitcast.317), channel_id=1, source_target_pairs={{0,8},{8,0},{16,24},{24,16},{32,40},{40,32},{48,56},{56,48},{64,72... | collective-permute-start | bytes 589832 | tf_op jit(solution)/shard_map/ppermute | solution.py:21
  151.7 15.8 %collective-permute-start.14 = (bf16[256,384]{0,1:T(8,128)(2,1)S(1)}, bf16[256,384]{0,1:T(8,128)(2,1)S(1)}, u32[]{:S(2)}, u32[]{:S(2)}) collective-permute-start(bf16[256,384]{0,1:T(8,128)(2,1)S(1)} %bitcast.315), channel_id=1, source_target_pairs={{0,32},{32,0},{8,40},{40,8},{16,48},{48,16},{24,56},{56,24},{64,96... | collective-permute-start | bytes 589832 | tf_op jit(solution)/shard_map/ppermute | solution.py:21
  155.8 11.7 %collective-permute-start.15 = (bf16[256,384]{0,1:T(8,128)(2,1)S(1)}, bf16[256,384]{0,1:T(8,128)(2,1)S(1)}, u32[]{:S(2)}, u32[]{:S(2)}) collective-permute-start(bf16[256,384]{0,1:T(8,128)(2,1)S(1)} %bitcast.316), channel_id=1, source_target_pairs={{0,64},{64,0},{8,72},{72,8},{16,80},{80,16},{24,88},{88,24},{32,96... | collective-permute-start | bytes 589832 | tf_op jit(solution)/shard_map/ppermute | solution.py:21
  159.1 22.2 %collective-permute-start.16 = (bf16[256,384]{0,1:T(8,128)(2,1)S(1)}, bf16[256,384]{0,1:T(8,128)(2,1)S(1)}, u32[]{:S(2)}, u32[]{:S(2)}) collective-permute-start(bf16[256,384]{0,1:T(8,128)(2,1)S(1)} %bitcast.318), channel_id=1, source_target_pairs={{0,128},{128,0},{8,136},{136,8},{16,144},{144,16},{24,152},{152,24... | collective-permute-start | bytes 589832 | tf_op jit(solution)/shard_map/ppermute | solution.py:21
  163.1 18.2 %collective-permute-start.17 = (bf16[256,384]{0,1:T(8,128)(2,1)}, bf16[256,384]{0,1:T(8,128)(2,1)}, u32[]{:S(2)}, u32[]{:S(2)}) collective-permute-start(bf16[256,384]{0,1:T(8,128)(2,1)} %bitcast.59), channel_id=1, source_target_pairs={{0,256},{256,0},{8,264},{264,8},{16,272},{272,16},{24,280},{280,24... | collective-permute-start | bytes 589832 | tf_op jit(solution)/shard_map/ppermute | solution.py:21
  (41 other events, 190.7 us)
where the time goes:
time: 203 us; the launch traced here: 201 us
  starting transfers between devices  79.3 us (39%)
  blocking collectives  37.3 us (18%)
  matrix products  31.5 us (16%)
  local copies, waits for them, and re-layouts  30.9 us (15%)
  waiting for transfers between devices  13.9 us (7%)
  other arithmetic  6.31 us (3%)
    ppermute x24, starting transfers between devices, swapped(): return lax.ppermute(block, axis, route)  79.3 us
    psum x1, blocking collectives, on_device(): lax.psum((jnp.sum(query_vals * query_vals, axis=1, keepdims=True), jnp.su...  23.2 us
    unnamed x104, local copies, waits for them, and re-layouts  19.1 us
    psum x1, blocking collectives, on_device(): lax.psum((jnp.sum(query_scaled * query_vals, axis=1, keepdims=True), jnp....  14.1 us
    ppermute x24, waiting for transfers between devices, swapped(): return lax.ppermute(block, axis, route)  13.9 us
    dot_general x7, matrix products, on_device(): jnp.einsum('hqk,khd->qhd', probs_list[band], value_list[band], preferred_...  13.2 us
    ppermute x6, local copies, waits for them, and re-layouts, swapped(): return lax.ppermute(block, axis, route)  10.5 us
    dot_general x7, matrix products, grad_terms(): jnp.einsum('hqk,qhd->khd', probs, grad_heads, preferred_element_type=jnp....  6.83 us
  transfers between devices with their start and end apart: 24, of which 1 were waited for; matrix products, arithmetic and copies ran while one was open for 21% of the time, Pallas kernels for 0%

commit v1 on v0

v1 whole, which is shorter than its diff:
```python
import functools
import math

import jax
import jax.numpy as jnp
from jax import lax
from jax.experimental import pallas as pl
from jax.experimental.pallas import tpu as pltpu
from jax.sharding import PartitionSpec as P

HD = 128
TILE = 128
BANDS = 7
EPS = 1e-06
NEG = -1e30
LOG2E = math.log2(math.e)
MESH = pl.DeviceIdType.MESH
F32 = jnp.float32
BF16 = jnp.bfloat16


def dot_nt(a, b, precision=None):
    return lax.dot_general(
        a, b, (((1,), (1,)), ((), ())), preferred_element_type=F32, precision=precision
    )


def dot_nn(a, b):
    return lax.dot_general(a, b, (((1,), (0,)), ((), ())), preferred_element_type=F32)


def columns_of(row, lanes=128):
    return jnp.broadcast_to(row, (lanes, row.shape[1])).T


def kernel(
    width,
    query_hbm,
    key_hbm,
    value_hbm,
    grad_hbm,
    query_gain,
    key_gain,
    bias,
    mask,
    att_out,
    dq_out,
    dk_out,
    dv_out,
    slab,
    fact,
    stat,
    zbuf,
    qt,
    kt,
    colq,
    colk,
    sbuf,
    pbuf,
    mrun,
    acc,
    dq,
    dk,
    dv,
    stage,
    load_sem,
    store_sem,
    send_sem,
    recv_sem,
    fact_send,
    fact_recv,
    stat_send,
    stat_recv,
    z_send,
    z_recv,
):
    heads = 3
    scale = HD**-0.5
    ctx = lax.axis_index("ctx")
    z = lax.axis_index("head")
    core = lax.rem(ctx, 2)
    x = lax.rem(ctx // 2, 4)
    y = ctx // 8
    tx = 1 - 2 * lax.rem(x, 2)
    t = 1 - 2 * lax.rem(y, 2)
    s = 1 - 2 * lax.rem(y // 2, 2)
    turns = s != t

    def dev(xn, yn, cn=core):
        return ((lax.rem(yn + 16, 8) * 4 + lax.rem(xn + 8, 4)) * 2 + cn, z)

    p_core = dev(x, y, 1 - core)
    p_x1 = dev(x + tx, y)
    p_xm = dev(x - tx, y)
    p_x2 = dev(x + 2, y)
    p_y1 = dev(x, y + t)
    p_ym = dev(x, y - t)
    p_ys = dev(x, y + s)
    p_y2 = dev(x, y + 2 * s)
    p_ym2 = dev(x, y - 2 * s)
    p_y4 = dev(x, y + 4)
    partners = [p_core, p_x1, p_x2, p_y1, p_y2, p_y4]
    z_peers = [(ctx, lax.rem(z + d, 8)) for d in range(1, 8)]

    hbm = [key_hbm, value_hbm, query_hbm, grad_hbm]

    def load(n):
        if n < 6:
            array, h = n % 2, n // 2
        else:
            array, h = 2 + n % 2, (n - 6) // 2
        return pltpu.make_async_copy(
            hbm[array].at[:, pl.ds(h * HD, HD)], slab.at[0, n], load_sem.at[n]
        )

    for n in (0, 1, 6, 2, 8, 4, 10, 3, 5, 7, 9, 11):
        load(n).start()

    barrier = pltpu.get_barrier_semaphore()
    peers = [p_core, p_x1, p_xm, p_x2, p_y1, p_ym, p_y2, p_ym2, p_y4] + z_peers
    for peer in peers:
        pl.semaphore_signal(barrier, inc=1, device_id=peer, device_id_type=MESH)
    pl.semaphore_wait(barrier, len(peers))

    def move(src, dst, n, way, to):
        return pltpu.make_async_remote_copy(
            src_ref=slab.at[src, n],
            dst_ref=slab.at[dst, n],
            send_sem=send_sem.at[way],
            recv_sem=recv_sem.at[dst, n],
            device_id=to,
            device_id_type=MESH,
        )

    def arrived(dst, n):
        move(0, dst, n, 0, p_core).wait_recv()

    def send_own(n):
        move(0, 4, n, 3, p_y1).start()

        @pl.when(turns)
        def _():
            move(0, 5, n, 4, p_y2).start()

        move(0, 2, n, 1, p_x1).start()
        move(0, 1, n, 0, p_core).start()

    def relay(n):
        arrived(4, n)

        @pl.when(turns)
        def _():
            move(4, 5, n, 5, p_ys).start()

        arrived(2, n)
        move(2, 3, n, 2, p_xm).start()

    def relay_far(n):
        arrived(5, n)
        move(5, 6, n, 6, p_ym2).start()

    def z_move(phase, d):
        return pltpu.make_async_remote_copy(
            src_ref=zbuf.at[phase, 0],
            dst_ref=zbuf.at[phase, d],
            send_sem=z_send.at[phase, d],
            recv_sem=z_recv.at[phase, d],
            device_id=z_peers[d - 1],
            device_id_type=MESH,
        )

    def z_sum(phase):
        total = zbuf[phase, 0]
        for d in range(1, 8):
            z_move(phase, d).wait_recv()
            total = total + zbuf[phase, d]
        return total

    def small_move(buf, send, recv, band):
        return pltpu.make_async_remote_copy(
            src_ref=buf.at[0],
            dst_ref=buf.at[band],
            send_sem=send.at[band],
            recv_sem=recv.at[band],
            device_id=partners[band - 1],
            device_id_type=MESH,
        )

    fact_move = functools.partial(small_move, fact, fact_send, fact_recv)
    stat_move = functools.partial(small_move, stat, stat_send, stat_recv)

    for n in range(6):
        load(n).wait()
        send_own(n)
    for n in range(6, 12):
        load(n).wait()

    ones = jnp.ones((8, HD), F32)
    row_id = lax.broadcasted_iota(jnp.int32, (8, 2 * TILE), 0)

    query_sq = jnp.zeros((8, 2 * TILE), F32)
    key_sq = jnp.zeros((8, 2 * TILE), F32)
    for h in range(heads):
        q_vals = slab[0, 6 + 2 * h].astype(F32)
        k_vals = slab[0, 2 * h].astype(F32)
        query_sq += dot_nt(ones, q_vals * q_vals, lax.Precision.HIGHEST)
        key_sq += dot_nt(ones, k_vals * k_vals, lax.Precision.HIGHEST)
    zbuf[0, 0] = jnp.where(row_id == 0, query_sq, key_sq)
    for d in range(1, 8):
        z_move(0, d).start()
    fact[0] = lax.rsqrt(z_sum(0) / width + EPS)
    for band in range(1, BANDS):
        fact_move(band).start()
    colq[...] = columns_of(fact[0, 0:1, :])
    colk[...] = columns_of(fact[0, 1:2, :])

    def gain_of(h):
        cols = pl.ds(h * HD, HD)
        return (query_gain[cols] * key_gain[cols] * scale)[None, :]

    for h in range(heads):
        both = gain_of(h) * LOG2E
        qt[h] = (slab[0, 6 + 2 * h].astype(F32) * colq[...] * both).astype(BF16)
        kt[h] = (slab[0, 2 * h].astype(F32) * colk[...] * both).astype(BF16)

    def shift_of(b, h, r, c):
        return jnp.where(mask[r, b, c] > 0, bias[b, h] * LOG2E, NEG)

    halves = [slice(0, TILE), slice(TILE, 2 * TILE)]

    def score_bands(h, low, high):
        def body(b, carry):
            factor = fact[b, 1:2, :]
            for r in range(2):
                scores = dot_nt(qt[h, halves[r], :], slab[b, 2 * h])
                top = mrun[halves[r], :]
                for c in range(2):
                    part = scores[:, halves[c]] * factor[:, halves[c]] + shift_of(b, h, r, c)
                    sbuf[b, halves[r], halves[c]] = part
                    top = jnp.maximum(top, part)
                mrun[halves[r], :] = top
            return carry

        lax.fori_loop(low, high, body, 0)

    def forward(h):
        top = jnp.max(mrun[...], axis=1, keepdims=True)
        acc[...] = jnp.zeros_like(acc)

        def exp_band(b, carry):
            for r in range(2):
                total = acc[halves[r], :]
                for c in range(2):
                    e = jnp.exp2(sbuf[b, halves[r], halves[c]] - top[halves[r], :])
                    sbuf[b, halves[r], halves[c]] = e
                    total = total + e
                acc[halves[r], :] = total
            return carry

        lax.fori_loop(0, BANDS, exp_band, 0)
        total = jnp.sum(acc[...], axis=1, keepdims=True)
        inverse = 1.0 / total
        lse = top + jnp.log(total) * LOG2E
        acc[...] = jnp.zeros_like(acc)

        def out_band(b, carry):
            for r in range(2):
                p = (sbuf[b, halves[r], :] * inverse[halves[r], :]).astype(BF16)
                pbuf[b, halves[r], :] = p
                acc[halves[r], :] += dot_nn(p, slab[b, 2 * h + 1])
            return carry

        lax.fori_loop(0, BANDS, out_band, 0)
        att = acc[...].astype(BF16)
        stage[0, h] = att
        store(0, h).start()
        delta = jnp.sum(slab[0, 7 + 2 * h].astype(F32) * att.astype(F32), axis=1, keepdims=True)
        stat[0, h : h + 1, :] = jnp.broadcast_to(lse, (2 * TILE, TILE)).T[0:1, :]
        stat[0, 3 + h : 4 + h, :] = jnp.broadcast_to(delta, (2 * TILE, TILE)).T[0:1, :]
        dq[h] = jnp.zeros_like(acc)

        def grad_band(b, carry):
            factor = fact[b, 1:2, :]
            for r in range(2):
                dp = dot_nt(slab[0, 7 + 2 * h, halves[r], :], slab[b, 2 * h + 1])
                p = pbuf[b, halves[r], :].astype(F32)
                ds = (p * (dp - delta[halves[r], :]) * factor).astype(BF16)
                dq[h, halves[r], :] += dot_nn(ds, slab[b, 2 * h])
            return carry

        lax.fori_loop(0, BANDS, grad_band, 0)

    def key_bands(h, low, high):
        def body(b, carry):
            factor = fact[b, 0:1, :]
            lse = stat[b, h : h + 1, :]
            delta = stat[b, 3 + h : 4 + h, :]
            for r in range(2):
                scores = dot_nt(kt[h, halves[r], :], slab[b, 6 + 2 * h])
                parts = []
                for c in range(2):
                    rest = shift_of(b, h, r, c) - lse[:, halves[c]]
                    parts.append(jnp.exp2(scores[:, halves[c]] * factor[:, halves[c]] + rest))
                p = jnp.concatenate(parts, axis=1)
                dv[h, halves[r], :] += dot_nn(p.astype(BF16), slab[b, 7 + 2 * h])
                dp = dot_nt(slab[0, 2 * h + 1, halves[r], :], slab[b, 7 + 2 * h])
                ds = (p * (dp - delta) * factor).astype(BF16)
                dk[h, halves[r], :] += dot_nn(ds, slab[b, 6 + 2 * h])
            return carry

        lax.fori_loop(low, high, body, 0)

    outs = [att_out, dq_out, dk_out, dv_out]

    def store(which, h):
        return pltpu.make_async_copy(
            stage.at[which, h], outs[which].at[:, pl.ds(h * HD, HD)], store_sem.at[which, h]
        )

    def inner_start(phase, total, base):
        inner = jnp.zeros((8, 2 * TILE), F32)
        for h in range(heads):
            scaled = total[h] * gain_of(h)
            total[h] = scaled
            inner += dot_nt(
                ones, scaled * slab[0, base + 2 * h].astype(F32), lax.Precision.HIGHEST
            )
        zbuf[phase, 0] = inner
        for d in range(1, 8):
            z_move(phase, d).start()

    def inner_finish(phase, total, base, col, which):
        inner = columns_of(z_sum(phase)[0:1, :] / width)
        factor = col[...]
        cubed = factor * factor * factor * inner
        for h in range(heads):
            vals = slab[0, base + 2 * h].astype(F32)
            stage[which, h] = (factor * total[h] - vals * cubed).astype(BF16)
            store(which, h).start()

    def fresh():
        mrun[...] = jnp.full(mrun.shape, NEG, F32)

    def near(n):
        arrived(1, n)
        arrived(3, n)

    dk[...] = jnp.zeros_like(dk)
    dv[...] = jnp.zeros_like(dv)
    for h in range(heads):
        n = 2 * h
        if h == 0:
            relay(0)
            relay(1)
            relay_far(0)
        relay(n + 2)
        relay_far(n + 1)
        send_own(6 + 2 * h)
        if h == 0:
            for band in range(1, BANDS):
                fact_move(band).wait_recv()
        fresh()
        near(n)
        score_bands(h, 0, 6)
        relay(n + 3)
        relay_far(n + 2)
        send_own(7 + 2 * h)
        near(n + 1)
        arrived(6, n)
        score_bands(h, 6, 7)
        arrived(6, n + 1)
        forward(h)
    for band in range(1, BANDS):
        stat_move(band).start()
    inner_start(1, dq, 6)
    for h in range(heads):
        n = 6 + 2 * h
        if n + 2 < 12:
            relay(n + 2)
        relay_far(n + 1)
        if h == 0:
            for band in range(1, BANDS):
                stat_move(band).wait_recv()
        near(n)
        near(n + 1)
        key_bands(h, 0, 6)
        if n + 2 < 12:
            relay(n + 3)
            relay_far(n + 2)
        if h == 0:
            inner_finish(1, dq, 6, colq, 1)
        arrived(6, n)
        arrived(6, n + 1)
        key_bands(h, 6, 7)
        stage[3, h] = dv[h].astype(BF16)
        store(3, h).start()
    inner_start(2, dk, 0)
    inner_finish(2, dk, 0, colk, 2)

    for which in range(4):
        for h in range(heads):
            store(which, h).wait()
    for phase in range(3):
        for d in range(1, 8):
            z_move(phase, d).wait_send()
    for band in range(1, BANDS):
        fact_move(band).wait_send()
        stat_move(band).wait_send()

    def sent(way):
        pltpu.make_async_remote_copy(
            src_ref=slab.at[0],
            dst_ref=slab.at[1],
            send_sem=send_sem.at[way],
            recv_sem=recv_sem.at[1, 0],
            device_id=p_core,
            device_id_type=MESH,
        ).wait_send()

    for way in (0, 1, 2, 3, 6):
        sent(way)

    @pl.when(turns)
    def _():
        sent(4)
        sent(5)


def on_device(query_proj, key_proj, value, out_grad, query_gain, key_gain, band_bias, tile_mask):
    rows, cols = query_proj.shape
    width = cols * lax.axis_size("head")
    hbm = pl.BlockSpec(memory_space=pl.ANY)
    vmem = pl.BlockSpec(memory_space=pltpu.VMEM)
    smem = pl.BlockSpec(memory_space=pltpu.SMEM)
    heads = cols // HD
    return pl.pallas_call(
        functools.partial(kernel, width),
        out_shape=[jax.ShapeDtypeStruct((rows, cols), BF16)] * 4,
        in_specs=[hbm] * 4 + [vmem] * 2 + [smem] * 2,
        out_specs=[hbm] * 4,
        scratch_shapes=[
            pltpu.VMEM((BANDS, 4 * heads, rows, HD), BF16),
            pltpu.VMEM((BANDS, 8, rows), F32),
            pltpu.VMEM((BANDS, 8, rows), F32),
            pltpu.VMEM((3, 8, 8, rows), F32),
            pltpu.VMEM((heads, rows, HD), BF16),
            pltpu.VMEM((heads, rows, HD), BF16),
            pltpu.VMEM((rows, TILE), F32),
            pltpu.VMEM((rows, TILE), F32),
            pltpu.VMEM((BANDS, rows, rows), F32),
            pltpu.VMEM((BANDS, rows, rows), BF16),
            pltpu.VMEM((rows, TILE), F32),
            pltpu.VMEM((rows, TILE), F32),
            pltpu.VMEM((heads, rows, HD), F32),
            pltpu.VMEM((heads, rows, HD), F32),
            pltpu.VMEM((heads, rows, HD), F32),
            pltpu.VMEM((4, heads, rows, HD), BF16),
            pltpu.SemaphoreType.DMA((4 * heads,)),
            pltpu.SemaphoreType.DMA((4, heads)),
            pltpu.SemaphoreType.DMA((7,)),
            pltpu.SemaphoreType.DMA((BANDS, 4 * heads)),
            pltpu.SemaphoreType.DMA((BANDS,)),
            pltpu.SemaphoreType.DMA((BANDS,)),
            pltpu.SemaphoreType.DMA((BANDS,)),
            pltpu.SemaphoreType.DMA((BANDS,)),
            pltpu.SemaphoreType.DMA((3, 8)),
            pltpu.SemaphoreType.DMA((3, 8)),
        ],
        compiler_params=pltpu.CompilerParams(
            collective_id=0, has_side_effects=True, vmem_limit_bytes=40 * 2**20
        ),
    )(query_proj, key_proj, value, out_grad, query_gain, key_gain, band_bias, tile_mask)


def solution(mesh):
    placed = (
        P("ctx", "head"),
        P("ctx", "head"),
        P("ctx", "head"),
        P("ctx", "head"),
        P("head"),
        P("head"),
        P(None, "head"),
        P("ctx", None, None),
    )
    return jax.shard_map(
        on_device,
        mesh=mesh,
        in_specs=placed,
        out_specs=(P("ctx", "head"), P("ctx", "head"), P("ctx", "head"), P("ctx", "head")),
        check_vma=False,
    )
```

time: 203 us -> 105 us (0.52)
  Pallas kernels: 0 us -> 95.7 us
  starting transfers between devices: 79.3 us -> 0 us
  blocking collectives: 37.3 us -> 0 us
  matrix products: 31.5 us -> 0 us
  local copies, waits for them, and re-layouts: 30.9 us -> 7.89 us
  waiting for transfers between devices: 13.9 us -> 0 us
  other arithmetic: 6.31 us -> 0 us
    pallas_call x0 -> x1, Pallas kernels: none -> 95.7 us  [on_device(): pl.pallas_call(functools.partial(kernel, width), out_shape=[jax.ShapeDtyp...]
    ppermute x24 -> x0, starting transfers between devices: 79.3 us -> none  [swapped(): return lax.ppermute(block, axis, route)]
    psum x2 -> x0, blocking collectives: 37.3 us -> none  [the longest x1 23.2 us: on_device(): lax.psum((jnp.sum(query_vals * query_vals, axis=1, keepdims=True), jnp.su...]
    dot_general x42 -> x0, matrix products: 31.5 us -> none  [the longest x7 13.2 us: on_device(): jnp.einsum('hqk,khd->qhd', probs_list[band], value_list[band], preferred_...]
    ppermute x24 -> x0, waiting for transfers between devices: 13.9 us -> none  [swapped(): return lax.ppermute(block, axis, route)]
    unnamed x104 -> x20, local copies, waits for them, and re-layouts: 19.1 us -> 7.89 us
    ppermute x6 -> x0, local copies, waits for them, and re-layouts: 10.5 us -> none  [swapped(): return lax.ppermute(block, axis, route)]
    convert_element_type x6 -> x0, other arithmetic: 2.67 us -> none  [the longest x1 1.45 us: on_device(): value_acc.reshape(rows, -1).astype(jnp.bfloat16)]
  transfers between devices with their start and end apart: 24 -> 0, of which waited for: 1 -> 0; matrix products, arithmetic and copies ran while one was open for 21% -> 0% of each run, Pallas kernels for 0% -> 0%
where the time goes in v1:
time: 105 us; the launch traced here: 104 us
  Pallas kernels  95.7 us (91%)
  local copies, waits for them, and re-layouts  7.89 us (8%)
    pallas_call x1, Pallas kernels, on_device(): pl.pallas_call(functools.partial(kernel, width), out_shape=[jax.ShapeDtyp...  95.7 us
    unnamed x20, local copies, waits for them, and re-layouts  7.89 us

profile of v1, /device:TPU:6, one launch (start us, length us, event | category | flops | bytes accessed | tf_op | source)
XLA Modules:
  0.0 104.3 jit_solution(4663073644003143249)
XLA Ops:
  0.6 0.0 copy-start.6
  0.6 0.8 copy.12.bias
  1.4 0.0 copy-done.6
  1.4 0.0 copy-start.4
  1.4 0.0 copy-start.5
  1.4 0.1 copy.13.mask
  1.5 0.6 copy-done.4
  2.1 0.0 copy-done.5
  2.1 0.0 copy-start
  2.1 0.9 copy-done
  3.0 0.0 copy-start.1
  3.0 0.9 copy-done.1
  4.0 0.0 copy-start.2
  4.0 0.9 copy-done.2
  4.9 0.0 copy-start.3
  4.9 0.9 copy-done.3
  5.8 95.7 %shard_map.111 = (bf16[256,384]{1,0:T(8,128)(2,1)S(1)}, bf16[256,384]{1,0:T(8,128)(2,1)S(1)}, bf16[256,384]{1,0:T(8,128)(2,1)S(1)}, bf16[256,384]{1,0:T(8,128)(2,1)S(1)}) custom-call(bf16[256,384]{1,0:T(8,128)(2,1)S(1)} %copy-done, bf16[256,384]{1,0:T(8,128)(2,1)S(1)} %copy-done.1, bf16[256,384]{1,0:T(8,128)(2,1)S(1)} %copy-done.2, ...), custom_call_target="tpu_custom_call" | custom-call | tf_op jit(solution)/shard_map/pallas_call | solution.py:436
  101.6 0.7 copy.18
  102.3 0.7 copy.19
  102.9 0.7 copy.20
  103.6 0.7 copy.21
Async XLA Ops:
  0.6 0.8 copy-start.6
  1.4 0.7 copy-start.4
  1.4 0.7 copy-start.5
  2.1 0.9 copy-start
  3.0 0.9 copy-start.1
  4.0 0.9 copy-start.2
  4.9 0.9 copy-start.3

commit v2 on v1

--- a/solution.py
+++ b/solution.py
@@ -11,6 +11,7 @@
 HD = 128
 TILE = 128
 BANDS = 7
+WINDOW = 3
 EPS = 1e-06
 NEG = -1e30
 LOG2E = math.log2(math.e)
@@ -189,10 +190,10 @@
     fact_move = functools.partial(small_move, fact, fact_send, fact_recv)
     stat_move = functools.partial(small_move, stat, stat_send, stat_recv)
 
-    for n in range(6):
+    for n in range(WINDOW):
         load(n).wait()
         send_own(n)
-    for n in range(6, 12):
+    for n in range(WINDOW, 12):
         load(n).wait()
 
     ones = jnp.ones((8, HD), F32)
@@ -208,23 +209,23 @@
     zbuf[0, 0] = jnp.where(row_id == 0, query_sq, key_sq)
     for d in range(1, 8):
         z_move(0, d).start()
-    fact[0] = lax.rsqrt(z_sum(0) / width + EPS)
-    for band in range(1, BANDS):
-        fact_move(band).start()
-    colq[...] = columns_of(fact[0, 0:1, :])
-    colk[...] = columns_of(fact[0, 1:2, :])
-
     def gain_of(h):
         cols = pl.ds(h * HD, HD)
         return (query_gain[cols] * key_gain[cols] * scale)[None, :]
 
-    for h in range(heads):
-        both = gain_of(h) * LOG2E
-        qt[h] = (slab[0, 6 + 2 * h].astype(F32) * colq[...] * both).astype(BF16)
-        kt[h] = (slab[0, 2 * h].astype(F32) * colk[...] * both).astype(BF16)
+    def factors():
+        fact[0] = lax.rsqrt(z_sum(0) / width + EPS)
+        for band in range(1, BANDS):
+            fact_move(band).start()
+        colq[...] = columns_of(fact[0, 0:1, :])
+        colk[...] = columns_of(fact[0, 1:2, :])
+        for h in range(heads):
+            both = gain_of(h) * LOG2E
+            qt[h] = (slab[0, 6 + 2 * h].astype(F32) * colq[...] * both).astype(BF16)
+            kt[h] = (slab[0, 2 * h].astype(F32) * colk[...] * both).astype(BF16)
 
     def shift_of(b, h, r, c):
-        return jnp.where(mask[r, b, c] > 0, bias[b, h] * LOG2E, NEG)
+        return jnp.where(mask[r, c, b] > 0, bias[h, b] * LOG2E, NEG)
 
     halves = [slice(0, TILE), slice(TILE, 2 * TILE)]
 
@@ -241,7 +242,7 @@
                 mrun[halves[r], :] = top
             return carry
 
-        lax.fori_loop(low, high, body, 0)
+        lax.fori_loop(low, high, body, 0, unroll=True)
 
     def forward(h):
         top = jnp.max(mrun[...], axis=1, keepdims=True)
@@ -257,7 +258,7 @@
                 acc[halves[r], :] = total
             return carry
 
-        lax.fori_loop(0, BANDS, exp_band, 0)
+        lax.fori_loop(0, BANDS, exp_band, 0, unroll=True)
         total = jnp.sum(acc[...], axis=1, keepdims=True)
         inverse = 1.0 / total
         lse = top + jnp.log(total) * LOG2E
@@ -270,7 +271,7 @@
                 acc[halves[r], :] += dot_nn(p, slab[b, 2 * h + 1])
             return carry
 
-        lax.fori_loop(0, BANDS, out_band, 0)
+        lax.fori_loop(0, BANDS, out_band, 0, unroll=True)
         att = acc[...].astype(BF16)
         stage[0, h] = att
         store(0, h).start()
@@ -288,7 +289,7 @@
                 dq[h, halves[r], :] += dot_nn(ds, slab[b, 2 * h])
             return carry
 
-        lax.fori_loop(0, BANDS, grad_band, 0)
+        lax.fori_loop(0, BANDS, grad_band, 0, unroll=True)
 
     def key_bands(h, low, high):
         def body(b, carry):
@@ -308,7 +309,7 @@
                 dk[h, halves[r], :] += dot_nn(ds, slab[b, 6 + 2 * h])
             return carry
 
-        lax.fori_loop(low, high, body, 0)
+        lax.fori_loop(low, high, body, 0, unroll=True)
 
     outs = [att_out, dq_out, dk_out, dv_out]
 
@@ -317,15 +318,15 @@
             stage.at[which, h], outs[which].at[:, pl.ds(h * HD, HD)], store_sem.at[which, h]
         )
 
-    def inner_start(phase, total, base):
-        inner = jnp.zeros((8, 2 * TILE), F32)
-        for h in range(heads):
-            scaled = total[h] * gain_of(h)
-            total[h] = scaled
-            inner += dot_nt(
-                ones, scaled * slab[0, base + 2 * h].astype(F32), lax.Precision.HIGHEST
-            )
-        zbuf[phase, 0] = inner
+    def inner_add(phase, total, base, h):
+        scaled = total[h] * gain_of(h)
+        total[h] = scaled
+        part = dot_nt(ones, scaled * slab[0, base + 2 * h].astype(F32), lax.Precision.HIGHEST)
+        if h > 0:
+            part += zbuf[phase, 0]
+        zbuf[phase, 0] = part
+
+    def inner_start(phase):
         for d in range(1, 8):
             z_move(phase, d).start()
 
@@ -338,63 +339,57 @@
             stage[which, h] = (factor * total[h] - vals * cubed).astype(BF16)
             store(which, h).start()
 
-    def fresh():
-        mrun[...] = jnp.full(mrun.shape, NEG, F32)
-
-    def near(n):
-        arrived(1, n)
-        arrived(3, n)
-
     dk[...] = jnp.zeros_like(dk)
     dv[...] = jnp.zeros_like(dv)
-    for h in range(heads):
-        n = 2 * h
-        if h == 0:
-            relay(0)
-            relay(1)
-            relay_far(0)
-        relay(n + 2)
-        relay_far(n + 1)
-        send_own(6 + 2 * h)
-        if h == 0:
+
+    def all_here(n):
+        for k in (n, n + 1):
+            arrived(1, k)
+            arrived(3, k)
+            arrived(6, k)
+
+    def query_side(h):
+        all_here(2 * h)
+        mrun[...] = jnp.full(mrun.shape, NEG, F32)
+        score_bands(h, 0, BANDS)
+        forward(h)
+        inner_add(1, dq, 6, h)
+
+    for n in range(12):
+        relay(n)
+        if n > 0:
+            relay_far(n - 1)
+        if n + WINDOW < 12:
+            send_own(n + WINDOW)
+        if n == 1:
+            factors()
+        if n == 3:
             for band in range(1, BANDS):
                 fact_move(band).wait_recv()
-        fresh()
-        near(n)
-        score_bands(h, 0, 6)
-        relay(n + 3)
-        relay_far(n + 2)
-        send_own(7 + 2 * h)
-        near(n + 1)
-        arrived(6, n)
-        score_bands(h, 6, 7)
-        arrived(6, n + 1)
-        forward(h)
+        if n in (4, 6, 8):
+            query_side(n // 2 - 2)
+        if n == 8:
+            for band in range(1, BANDS):
+                stat_move(band).start()
+            inner_start(1)
+        if n == 10:
+            inner_finish(1, dq, 6, colq, 1)
+    relay_far(11)
     for band in range(1, BANDS):
-        stat_move(band).start()
-    inner_start(1, dq, 6)
+        stat_move(band).wait_recv()
     for h in range(heads):
         n = 6 + 2 * h
-        if n + 2 < 12:
-            relay(n + 2)
-        relay_far(n + 1)
-        if h == 0:
-            for band in range(1, BANDS):
-                stat_move(band).wait_recv()
-        near(n)
-        near(n + 1)
+        for k in (n, n + 1):
+            arrived(1, k)
+            arrived(3, k)
         key_bands(h, 0, 6)
-        if n + 2 < 12:
-            relay(n + 3)
-            relay_far(n + 2)
-        if h == 0:
-            inner_finish(1, dq, 6, colq, 1)
         arrived(6, n)
         arrived(6, n + 1)
         key_bands(h, 6, 7)
+        inner_add(2, dk, 0, h)
         stage[3, h] = dv[h].astype(BF16)
         store(3, h).start()
-    inner_start(2, dk, 0)
+    inner_start(2)
     inner_finish(2, dk, 0, colk, 2)
 
     for which in range(4):
@@ -426,6 +421,19 @@
         sent(5)
 
 
+def hand_over(*refs):
+    held, in_sem, out_sem = refs[8:]
+    here = [pltpu.make_async_copy(refs[i], held.at[i], in_sem.at[i]) for i in range(4)]
+    away = [pltpu.make_async_copy(held.at[i], refs[4 + i], out_sem.at[i]) for i in range(4)]
+    for copy in here:
+        copy.start()
+    for i in range(4):
+        here[i].wait()
+        away[i].start()
+    for copy in away:
+        copy.wait()
+
+
 def on_device(query_proj, key_proj, value, out_grad, query_gain, key_gain, band_bias, tile_mask):
     rows, cols = query_proj.shape
     width = cols * lax.axis_size("head")
@@ -433,7 +441,7 @@
     vmem = pl.BlockSpec(memory_space=pltpu.VMEM)
     smem = pl.BlockSpec(memory_space=pltpu.SMEM)
     heads = cols // HD
-    return pl.pallas_call(
+    outs = pl.pallas_call(
         functools.partial(kernel, width),
         out_shape=[jax.ShapeDtypeStruct((rows, cols), BF16)] * 4,
         in_specs=[hbm] * 4 + [vmem] * 2 + [smem] * 2,
@@ -467,9 +475,30 @@
             pltpu.SemaphoreType.DMA((3, 8)),
         ],
         compiler_params=pltpu.CompilerParams(
-            collective_id=0, has_side_effects=True, vmem_limit_bytes=40 * 2**20
+            collective_id=0, has_side_effects=True, vmem_limit_bytes=60 * 2**20
         ),
-    )(query_proj, key_proj, value, out_grad, query_gain, key_gain, band_bias, tile_mask)
+    )(
+        query_proj,
+        key_proj,
+        value,
+        out_grad,
+        query_gain,
+        key_gain,
+        band_bias.T,
+        tile_mask.transpose(0, 2, 1),
+    )
+    return pl.pallas_call(
+        hand_over,
+        out_shape=[jax.ShapeDtypeStruct((rows, cols), BF16)] * 4,
+        in_specs=[hbm] * 4,
+        out_specs=[hbm] * 4,
+        scratch_shapes=[
+            pltpu.VMEM((4, rows, cols), BF16),
+            pltpu.SemaphoreType.DMA((4,)),
+            pltpu.SemaphoreType.DMA((4,)),
+        ],
+        compiler_params=pltpu.CompilerParams(vmem_limit_bytes=60 * 2**20),
+    )(*outs)
 
 
 def solution(mesh):

time: 105 us -> 82.2 us (0.78)
  the two profiles are of different devices: /device:TPU:6 before, /device:TPU:8 now
where the time goes in v2:
time: 82.2 us; the launch traced here: 82 us
  Pallas kernels  81.4 us (99%)
    pallas_call x1, Pallas kernels, on_device(): pl.pallas_call(functools.partial(kernel, width), out_shape=[jax.ShapeDtyp...  79.4 us
    pallas_call x1, Pallas kernels, on_device(): pl.pallas_call(hand_over, out_shape=[jax.ShapeDtypeStruct((rows, cols), B...  1.96 us

profile of v2, /device:TPU:8, one launch (start us, length us, event | category | flops | bytes accessed | tf_op | source)
XLA Modules:
  0.0 82.0 jit_solution(11103571622695345961)
XLA Ops:
  0.6 79.4 %shard_map.111 = (bf16[256,384]{1,0:T(8,128)(2,1)}, bf16[256,384]{1,0:T(8,128)(2,1)}, bf16[256,384]{1,0:T(8,128)(2,1)}, bf16[256,384]{1,0:T(8,128)(2,1)}) custom-call(bf16[256,384]{1,0:T(8,128)(2,1)} %query_hbm.1, bf16[256,384]{1,0:T(8,128)(2,1)} %key_hbm.1, bf16[256,384]{1,0:T(8,128)(2,1)} %value_hbm.1, bf16[256,384]{1,0:T(8,128)(2,1)} %grad_hbm.1, ...), custom_call_target="tpu_custom_call" | custom-call | tf_op jit(solution)/shard_map/pallas_call | solution.py:444
  80.1 2.0 %shard_map.112 = (bf16[256,384]{1,0:T(8,128)(2,1)}, bf16[256,384]{1,0:T(8,128)(2,1)}, bf16[256,384]{1,0:T(8,128)(2,1)}, bf16[256,384]{1,0:T(8,128)(2,1)}) custom-call(bf16[256,384]{1,0:T(8,128)(2,1)} %get-tuple-element.8.refs_0_, bf16[256,384]{1,0:T(8,128)(2,1)} %get-tuple-element.9.refs_1_, bf16[256,384]{1,0:T(8,128)(2,1)} %get-tuple-element.10.refs_2_, ...), custom_call_target="tpu_custom_call" | custom-call | tf_op jit(solution)/shard_map/pallas_call | solution.py:490

commit v3 on v2

--- a/solution.py
+++ b/solution.py
@@ -11,7 +11,8 @@
 HD = 128
 TILE = 128
 BANDS = 7
-WINDOW = 3
+WINDOW = 2
+BACK = 1
 EPS = 1e-06
 NEG = -1e30
 LOG2E = math.log2(math.e)
@@ -28,6 +29,10 @@
 
 def dot_nn(a, b):
     return lax.dot_general(a, b, (((1,), (0,)), ((), ())), preferred_element_type=F32)
+
+
+def dot_tn(a, b):
+    return lax.dot_general(a, b, (((0,), (0,)), ((), ())), preferred_element_type=F32)
 
 
 def columns_of(row, lanes=128):
@@ -64,6 +69,11 @@
     dk,
     dv,
     stage,
+    part,
+    rin,
+    dsb,
+    back_send,
+    back_recv,
     load_sem,
     store_sem,
     send_sem,
@@ -136,6 +146,12 @@
     def arrived(dst, n):
         move(0, dst, n, 0, p_core).wait_recv()
 
+    main = list(range(6)) + list(range(6 + 2 * BACK, 12))
+
+    def send_side(n):
+        move(0, 2, n, 1, p_x1).start()
+        move(0, 1, n, 0, p_core).start()
+
     def send_own(n):
         move(0, 4, n, 3, p_y1).start()
 
@@ -143,8 +159,11 @@
         def _():
             move(0, 5, n, 4, p_y2).start()
 
-        move(0, 2, n, 1, p_x1).start()
-        move(0, 1, n, 0, p_core).start()
+        send_side(n)
+
+    def relay_side(n):
+        arrived(2, n)
+        move(2, 3, n, 2, p_xm).start()
 
     def relay(n):
         arrived(4, n)
@@ -153,8 +172,59 @@
         def _():
             move(4, 5, n, 5, p_ys).start()
 
-        arrived(2, n)
-        move(2, 3, n, 2, p_xm).start()
+        relay_side(n)
+
+    def back(src, kind, h, to):
+        return pltpu.make_async_remote_copy(
+            src_ref=part.at[src, h],
+            dst_ref=rin.at[kind, h],
+            send_sem=back_send.at[src, h],
+            recv_sem=back_recv.at[kind, h],
+            device_id=to,
+            device_id_type=MESH,
+        )
+
+    def joined(src, kind, h):
+        for c in range(2):
+            both = part[src, h, c].astype(F32) + rin[kind, h, c].astype(F32)
+            part[src, h, c] = both.astype(BF16)
+
+    def back_first(h):
+        back(2, 0, h, p_ym2).start()
+
+        @pl.when(jnp.logical_not(turns))
+        def _():
+            back(0, 3, h, p_y1).start()
+
+    def back_second(h):
+        back(2, 0, h, p_ym2).wait_recv()
+        joined(1, 0, h)
+
+        @pl.when(turns)
+        def _():
+            back(1, 1, h, p_ys).start()
+
+        @pl.when(jnp.logical_not(turns))
+        def _():
+            back(1, 2, h, p_y2).start()
+
+    def back_third(h):
+        @pl.when(turns)
+        def _():
+            back(1, 1, h, p_ys).wait_recv()
+            joined(0, 1, h)
+            back(0, 3, h, p_y1).start()
+
+    def back_last(h):
+        back(0, 3, h, p_y1).wait_recv()
+        dk[h] += rin[3, h, 0].astype(F32)
+        dv[h] += rin[3, h, 1].astype(F32)
+
+        @pl.when(turns)
+        def _():
+            back(1, 2, h, p_y2).wait_recv()
+            dk[h] += rin[2, h, 0].astype(F32)
+            dv[h] += rin[2, h, 1].astype(F32)
 
     def relay_far(n):
         arrived(5, n)
@@ -197,7 +267,6 @@
         load(n).wait()
 
     ones = jnp.ones((8, HD), F32)
-    row_id = lax.broadcasted_iota(jnp.int32, (8, 2 * TILE), 0)
 
     query_sq = jnp.zeros((8, 2 * TILE), F32)
     key_sq = jnp.zeros((8, 2 * TILE), F32)
@@ -206,7 +275,8 @@
         k_vals = slab[0, 2 * h].astype(F32)
         query_sq += dot_nt(ones, q_vals * q_vals, lax.Precision.HIGHEST)
         key_sq += dot_nt(ones, k_vals * k_vals, lax.Precision.HIGHEST)
-    zbuf[0, 0] = jnp.where(row_id == 0, query_sq, key_sq)
+    zbuf[0, 0, 0:1, :] = query_sq[0:1]
+    zbuf[0, 0, 1:2, :] = key_sq[0:1]
     for d in range(1, 8):
         z_move(0, d).start()
     def gain_of(h):
@@ -280,16 +350,26 @@
         stat[0, 3 + h : 4 + h, :] = jnp.broadcast_to(delta, (2 * TILE, TILE)).T[0:1, :]
         dq[h] = jnp.zeros_like(acc)
 
-        def grad_band(b, carry):
+        normed = (slab[0, 6 + 2 * h].astype(F32) * colq[...]).astype(BF16)
+
+        def grad_band(b):
             factor = fact[b, 1:2, :]
+            send_back = h < BACK and b >= 4
             for r in range(2):
                 dp = dot_nt(slab[0, 7 + 2 * h, halves[r], :], slab[b, 2 * h + 1])
                 p = pbuf[b, halves[r], :].astype(F32)
-                ds = (p * (dp - delta[halves[r], :]) * factor).astype(BF16)
-                dq[h, halves[r], :] += dot_nn(ds, slab[b, 2 * h])
-            return carry
-
-        lax.fori_loop(0, BANDS, grad_band, 0, unroll=True)
+                ds = p * (dp - delta[halves[r], :])
+                if send_back:
+                    dsb[halves[r], :] = ds.astype(BF16)
+                dq[h, halves[r], :] += dot_nn((ds * factor).astype(BF16), slab[b, 2 * h])
+            if send_back:
+                part[b - 4, h, 0] = dot_tn(dsb[...], normed).astype(BF16)
+                part[b - 4, h, 1] = dot_tn(pbuf[b], slab[0, 7 + 2 * h]).astype(BF16)
+
+        for b in reversed(range(BANDS)):
+            grad_band(b)
+            if h < BACK and b == 4:
+                back_first(h)
 
     def key_bands(h, low, high):
         def body(b, carry):
@@ -321,10 +401,10 @@
     def inner_add(phase, total, base, h):
         scaled = total[h] * gain_of(h)
         total[h] = scaled
-        part = dot_nt(ones, scaled * slab[0, base + 2 * h].astype(F32), lax.Precision.HIGHEST)
+        part = dot_nt(ones, scaled * slab[0, base + 2 * h].astype(F32), lax.Precision.HIGHEST)[0:1]
         if h > 0:
-            part += zbuf[phase, 0]
-        zbuf[phase, 0] = part
+            part += zbuf[phase, 0, 0:1, :]
+        zbuf[phase, 0, 0:1, :] = part[0:1]
 
     def inner_start(phase):
         for d in range(1, 8):
@@ -340,6 +420,8 @@
             store(which, h).start()
 
     dk[...] = jnp.zeros_like(dk)
+    zbuf[1, 0] = jnp.zeros((2, 2 * TILE), F32)
+    zbuf[2, 0] = jnp.zeros((2, 2 * TILE), F32)
     dv[...] = jnp.zeros_like(dv)
 
     def all_here(n):
@@ -355,26 +437,41 @@
         forward(h)
         inner_add(1, dq, 6, h)
 
-    for n in range(12):
-        relay(n)
-        if n > 0:
-            relay_far(n - 1)
-        if n + WINDOW < 12:
-            send_own(n + WINDOW)
-        if n == 1:
+    sides = list(range(6, 6 + 2 * BACK))
+    later = {}
+    for h in range(BACK):
+        later.setdefault(2 * h + 5, []).append(functools.partial(back_second, h))
+        later.setdefault(2 * h + 7, []).append(functools.partial(back_third, h))
+    for m in range(len(main)):
+        relay(main[m])
+        if m > 0:
+            relay_far(main[m - 1])
+        if m + WINDOW < len(main):
+            send_own(main[m + WINDOW])
+        if m > 2 and sides:
+            relay_side(sides.pop(0))
+        if 0 < m <= 2 * BACK:
+            send_side(5 + m)
+        if m == 1:
             factors()
-        if n == 3:
+        if m == 2:
             for band in range(1, BANDS):
                 fact_move(band).wait_recv()
-        if n in (4, 6, 8):
-            query_side(n // 2 - 2)
-        if n == 8:
+        for step in later.pop(m, []):
+            step()
+        if m in (3, 5, 7):
+            query_side((m - 3) // 2)
+        if m == 7:
             for band in range(1, BANDS):
                 stat_move(band).start()
             inner_start(1)
-        if n == 10:
-            inner_finish(1, dq, 6, colq, 1)
-    relay_far(11)
+    relay_far(main[-1])
+    for n in sides:
+        relay_side(n)
+    for m in sorted(later):
+        for step in later[m]:
+            step()
+    inner_finish(1, dq, 6, colq, 1)
     for band in range(1, BANDS):
         stat_move(band).wait_recv()
     for h in range(heads):
@@ -382,10 +479,14 @@
         for k in (n, n + 1):
             arrived(1, k)
             arrived(3, k)
-        key_bands(h, 0, 6)
-        arrived(6, n)
-        arrived(6, n + 1)
-        key_bands(h, 6, 7)
+        if h < BACK:
+            key_bands(h, 0, 4)
+            back_last(h)
+        else:
+            key_bands(h, 0, 6)
+            arrived(6, n)
+            arrived(6, n + 1)
+            key_bands(h, 6, 7)
         inner_add(2, dk, 0, h)
         stage[3, h] = dv[h].astype(BF16)
         store(3, h).start()
@@ -402,23 +503,29 @@
         fact_move(band).wait_send()
         stat_move(band).wait_send()
 
-    def sent(way):
+    def sent(way, count):
         pltpu.make_async_remote_copy(
-            src_ref=slab.at[0],
-            dst_ref=slab.at[1],
+            src_ref=slab.at[0, 0:count],
+            dst_ref=slab.at[1, 0:count],
             send_sem=send_sem.at[way],
             recv_sem=recv_sem.at[1, 0],
             device_id=p_core,
             device_id_type=MESH,
         ).wait_send()
 
-    for way in (0, 1, 2, 3, 6):
-        sent(way)
+    for way in (0, 1, 2):
+        sent(way, 12)
+    for way in (3, 6):
+        sent(way, len(main))
 
     @pl.when(turns)
     def _():
-        sent(4)
-        sent(5)
+        sent(4, len(main))
+        sent(5, len(main))
+
+    for h in range(BACK):
+        for src in range(3):
+            back(src, 0, h, p_y1).wait_send()
 
 
 def hand_over(*refs):
@@ -448,9 +555,9 @@
         out_specs=[hbm] * 4,
         scratch_shapes=[
             pltpu.VMEM((BANDS, 4 * heads, rows, HD), BF16),
+            pltpu.VMEM((BANDS, 2, rows), F32),
             pltpu.VMEM((BANDS, 8, rows), F32),
-            pltpu.VMEM((BANDS, 8, rows), F32),
-            pltpu.VMEM((3, 8, 8, rows), F32),
+            pltpu.VMEM((3, 8, 2, rows), F32),
             pltpu.VMEM((heads, rows, HD), BF16),
             pltpu.VMEM((heads, rows, HD), BF16),
             pltpu.VMEM((rows, TILE), F32),
@@ -463,6 +570,11 @@
             pltpu.VMEM((heads, rows, HD), F32),
             pltpu.VMEM((heads, rows, HD), F32),
             pltpu.VMEM((4, heads, rows, HD), BF16),
+            pltpu.VMEM((3, BACK, 2, rows, HD), BF16),
+            pltpu.VMEM((4, BACK, 2, rows, HD), BF16),
+            pltpu.VMEM((rows, rows), BF16),
+            pltpu.SemaphoreType.DMA((4, BACK)),
+            pltpu.SemaphoreType.DMA((4, BACK)),
             pltpu.SemaphoreType.DMA((4 * heads,)),
             pltpu.SemaphoreType.DMA((4, heads)),
             pltpu.SemaphoreType.DMA((7,)),

time: 82.2 us -> 78.7 us (0.957)
  the two profiles are of different devices: /device:TPU:8 before, /device:TPU:6 now
where the time goes in v3:
time: 78.7 us; the launch traced here: 77.6 us
  Pallas kernels  76.8 us (98%)
  between operations  0.8 us (1%)
    pallas_call x1, Pallas kernels, on_device(): pl.pallas_call(functools.partial(kernel, width), out_shape=[jax.ShapeDtyp...  74.8 us
    pallas_call x1, Pallas kernels, on_device(): pl.pallas_call(hand_over, out_shape=[jax.ShapeDtypeStruct((rows, cols), B...  1.96 us

profile of v3, /device:TPU:6, one launch (start us, length us, event | category | flops | bytes accessed | tf_op | source)
XLA Modules:
  0.0 77.6 jit_solution(109612794376179464)
XLA Ops:
  0.6 74.8 %shard_map.111 = (bf16[256,384]{1,0:T(8,128)(2,1)}, bf16[256,384]{1,0:T(8,128)(2,1)}, bf16[256,384]{1,0:T(8,128)(2,1)}, bf16[256,384]{1,0:T(8,128)(2,1)}) custom-call(bf16[256,384]{1,0:T(8,128)(2,1)} %query_hbm.1, bf16[256,384]{1,0:T(8,128)(2,1)} %key_hbm.1, bf16[256,384]{1,0:T(8,128)(2,1)} %value_hbm.1, bf16[256,384]{1,0:T(8,128)(2,1)} %grad_hbm.1, ...), custom_call_target="tpu_custom_call" | custom-call | tf_op jit(solution)/shard_map/pallas_call | solution.py:551
  75.5 2.0 %shard_map.112 = (bf16[256,384]{1,0:T(8,128)(2,1)}, bf16[256,384]{1,0:T(8,128)(2,1)}, bf16[256,384]{1,0:T(8,128)(2,1)}, bf16[256,384]{1,0:T(8,128)(2,1)}) custom-call(bf16[256,384]{1,0:T(8,128)(2,1)} %get-tuple-element.8.refs_0_, bf16[256,384]{1,0:T(8,128)(2,1)} %get-tuple-element.9.refs_1_, bf16[256,384]{1,0:T(8,128)(2,1)} %get-tuple-element.10.refs_2_, ...), custom_call_target="tpu_custom_call" | custom-call | tf_op jit(solution)/shard_map/pallas_call | solution.py:602

commit v4 on v3

--- a/solution.py
+++ b/solution.py
@@ -443,9 +443,9 @@
         later.setdefault(2 * h + 5, []).append(functools.partial(back_second, h))
         later.setdefault(2 * h + 7, []).append(functools.partial(back_third, h))
     for m in range(len(main)):
-        relay(main[m])
         if m > 0:
             relay_far(main[m - 1])
+        relay(main[m])
         if m + WINDOW < len(main):
             send_own(main[m + WINDOW])
         if m > 2 and sides:
@@ -465,31 +465,41 @@
             for band in range(1, BANDS):
                 stat_move(band).start()
             inner_start(1)
-    relay_far(main[-1])
-    for n in sides:
-        relay_side(n)
-    for m in sorted(later):
-        for step in later[m]:
-            step()
-    inner_finish(1, dq, 6, colq, 1)
-    for band in range(1, BANDS):
+        if m == 8:
+            for h in range(heads):
+                key_bands(h, 0, 1)
+            inner_finish(1, dq, 6, colq, 1)
+    assert not sides and not later
+    for band in range(1, 4):
         stat_move(band).wait_recv()
-    for h in range(heads):
-        n = 6 + 2 * h
-        for k in (n, n + 1):
+
+    def near(h):
+        for k in (6 + 2 * h, 7 + 2 * h):
             arrived(1, k)
             arrived(3, k)
-        if h < BACK:
-            key_bands(h, 0, 4)
-            back_last(h)
-        else:
-            key_bands(h, 0, 6)
-            arrived(6, n)
-            arrived(6, n + 1)
-            key_bands(h, 6, 7)
+
+    def key_done(h):
         inner_add(2, dk, 0, h)
         stage[3, h] = dv[h].astype(BF16)
         store(3, h).start()
+
+    for h in range(BACK):
+        near(h)
+        key_bands(h, 1, 4)
+    relay_far(main[-1])
+    for h in range(BACK):
+        back_last(h)
+        key_done(h)
+    for band in range(4, BANDS):
+        stat_move(band).wait_recv()
+    for h in range(BACK, heads):
+        n = 6 + 2 * h
+        near(h)
+        key_bands(h, 1, 6)
+        arrived(6, n)
+        arrived(6, n + 1)
+        key_bands(h, 6, 7)
+        key_done(h)
     inner_start(2)
     inner_finish(2, dk, 0, colk, 2)
 

time: 78.7 us -> 78.1 us (level)
  no operation moved by 1% of the time
where the time goes in v4:
time: 78.1 us; the launch traced here: 77.7 us
  Pallas kernels  76.9 us (98%)
  between operations  0.8 us (1%)
    pallas_call x1, Pallas kernels, on_device(): pl.pallas_call(functools.partial(kernel, width), out_shape=[jax.ShapeDtyp...  75 us
    pallas_call x1, Pallas kernels, on_device(): pl.pallas_call(hand_over, out_shape=[jax.ShapeDtypeStruct((rows, cols), B...  1.96 us

profile of v4, /device:TPU:6, one launch (start us, length us, event | category | flops | bytes accessed | tf_op | source)
XLA Modules:
  0.0 77.7 jit_solution(6890470920511035596)
XLA Ops:
  0.6 75.0 %shard_map.111 = (bf16[256,384]{1,0:T(8,128)(2,1)}, bf16[256,384]{1,0:T(8,128)(2,1)}, bf16[256,384]{1,0:T(8,128)(2,1)}, bf16[256,384]{1,0:T(8,128)(2,1)}) custom-call(bf16[256,384]{1,0:T(8,128)(2,1)} %query_hbm.1, bf16[256,384]{1,0:T(8,128)(2,1)} %key_hbm.1, bf16[256,384]{1,0:T(8,128)(2,1)} %value_hbm.1, bf16[256,384]{1,0:T(8,128)(2,1)} %grad_hbm.1, ...), custom_call_target="tpu_custom_call" | custom-call | tf_op jit(solution)/shard_map/pallas_call | solution.py:561
  75.6 2.0 %shard_map.112 = (bf16[256,384]{1,0:T(8,128)(2,1)}, bf16[256,384]{1,0:T(8,128)(2,1)}, bf16[256,384]{1,0:T(8,128)(2,1)}, bf16[256,384]{1,0:T(8,128)(2,1)}) custom-call(bf16[256,384]{1,0:T(8,128)(2,1)} %get-tuple-element.8.refs_0_, bf16[256,384]{1,0:T(8,128)(2,1)} %get-tuple-element.9.refs_1_, bf16[256,384]{1,0:T(8,128)(2,1)} %get-tuple-element.10.refs_2_, ...), custom_call_target="tpu_custom_call" | custom-call | tf_op jit(solution)/shard_map/pallas_call | solution.py:612

commit v5 on v4

--- a/solution.py
+++ b/solution.py
@@ -124,13 +124,13 @@
             hbm[array].at[:, pl.ds(h * HD, HD)], slab.at[0, n], load_sem.at[n]
         )
 
+    barrier = pltpu.get_barrier_semaphore()
+    far_first = [z_peers[d - 1] for d in (4, 3, 5, 2, 6, 1, 7)]
+    peers = far_first + [p_y4, p_y2, p_ym2, p_x2, p_y1, p_ym, p_x1, p_xm, p_core]
+    for peer in peers:
+        pl.semaphore_signal(barrier, inc=1, device_id=peer, device_id_type=MESH)
     for n in (0, 1, 6, 2, 8, 4, 10, 3, 5, 7, 9, 11):
         load(n).start()
-
-    barrier = pltpu.get_barrier_semaphore()
-    peers = [p_core, p_x1, p_xm, p_x2, p_y1, p_ym, p_y2, p_ym2, p_y4] + z_peers
-    for peer in peers:
-        pl.semaphore_signal(barrier, inc=1, device_id=peer, device_id_type=MESH)
     pl.semaphore_wait(barrier, len(peers))
 
     def move(src, dst, n, way, to):
@@ -407,7 +407,7 @@
         zbuf[phase, 0, 0:1, :] = part[0:1]
 
     def inner_start(phase):
-        for d in range(1, 8):
+        for d in (4, 3, 5, 2, 6, 1, 7):
             z_move(phase, d).start()
 
     def inner_finish(phase, total, base, col, which):

time: 78.1 us -> 78 us (level)
  no operation moved by 1% of the time
where the time goes in v5:
time: 78 us; the launch traced here: 77.6 us
  Pallas kernels  76.8 us (98%)
  between operations  0.8 us (1%)
    pallas_call x1, Pallas kernels, on_device(): pl.pallas_call(functools.partial(kernel, width), out_shape=[jax.ShapeDtyp...  74.9 us
    pallas_call x1, Pallas kernels, on_device(): pl.pallas_call(hand_over, out_shape=[jax.ShapeDtypeStruct((rows, cols), B...  1.96 us

profile of v5, /device:TPU:6, one launch (start us, length us, event | category | flops | bytes accessed | tf_op | source)
XLA Modules:
  0.0 77.6 jit_solution(4970269397424934322)
XLA Ops:
  0.6 74.9 %shard_map.111 = (bf16[256,384]{1,0:T(8,128)(2,1)}, bf16[256,384]{1,0:T(8,128)(2,1)}, bf16[256,384]{1,0:T(8,128)(2,1)}, bf16[256,384]{1,0:T(8,128)(2,1)}) custom-call(bf16[256,384]{1,0:T(8,128)(2,1)} %query_hbm.1, bf16[256,384]{1,0:T(8,128)(2,1)} %key_hbm.1, bf16[256,384]{1,0:T(8,128)(2,1)} %value_hbm.1, bf16[256,384]{1,0:T(8,128)(2,1)} %grad_hbm.1, ...), custom_call_target="tpu_custom_call" | custom-call | tf_op jit(solution)/shard_map/pallas_call | solution.py:561
  75.5 2.0 %shard_map.112 = (bf16[256,384]{1,0:T(8,128)(2,1)}, bf16[256,384]{1,0:T(8,128)(2,1)}, bf16[256,384]{1,0:T(8,128)(2,1)}, bf16[256,384]{1,0:T(8,128)(2,1)}) custom-call(bf16[256,384]{1,0:T(8,128)(2,1)} %get-tuple-element.8.refs_0_, bf16[256,384]{1,0:T(8,128)(2,1)} %get-tuple-element.9.refs_1_, bf16[256,384]{1,0:T(8,128)(2,1)} %get-tuple-element.10.refs_2_, ...), custom_call_target="tpu_custom_call" | custom-call | tf_op jit(solution)/shard_map/pallas_call | solution.py:612
